TPU v7x, 32 devices: a whole 2x2x4 slice. The times are simulated.
32 devices in a mesh: grp: 2 (over x), lat: 16 (over z, y, core).
Axes of the slice: x: 2, y: 2, z: 4, core: 2. Of those that a mesh axis runs over, the one named last changes fastest.
Arguments:
- state_field: bfloat16 [8, 48, 180, 768], P('grp', 'lat'), parts along dimension 0, may hold values from -6 to 6
- norm1_gain: float32 [768], replicated, may hold values from 0.25 to 1.75
- norm1_shift: float32 [768], replicated, may hold values from -3 to 3
- spec_w1: bfloat16 [2, 8, 96, 96], replicated, may hold values from -0.4375 to 0.4375
- spec_b1: float32 [2, 768], replicated, may hold values from -3 to 3
- spec_w2: bfloat16 [2, 8, 96, 96], replicated, may hold values from -0.625 to 0.625
- spec_b2: float32 [2, 768], replicated, may hold values from -3 to 3
- norm2_gain: float32 [768], replicated, may hold values from 0.25 to 1.75
- norm2_shift: float32 [768], replicated, may hold values from -3 to 3
- fc1_weight: bfloat16 [768, 3072], replicated, may hold values from -0.21875 to 0.21875
- fc1_bias: float32 [3072], replicated, may hold values from -3 to 3
- fc2_weight: bfloat16 [3072, 768], replicated, may hold values from -0.109375 to 0.109375
- fc2_bias: float32 [768], replicated, may hold values from -3 to 3
Outputs:
- block_out: bfloat16 [8, 48, 180, 768], P('grp', 'lat'), parts along dimension 0
There are 2 independent parts, one for each index of `grp`. A program takes and returns all parts, laid end to end along the dimension named above; an argument that names none is the same for every part. Nothing has to cross between parts.
All inputs are finite; a program needn't handle non-finite values.
Results may differ from a plain program's by a relative error of at most 0.007.
Values may be sent and summed in bfloat16 or wider, within the bound.
No kernel may reach another device: no remote copies, remote signals or barrier semaphores. Data moves between devices by JAX's collectives and lax.ppermute only.
A program may use at most 128 MiB of HBM per device.

v0:
```python
import math

import jax
import jax.numpy as jnp
from jax import lax
from jax.sharding import PartitionSpec as P

KW = 64


def lon_tables(width, kept):
    along = jnp.arange(width, dtype=jnp.int32)
    waves = jnp.arange(kept, dtype=jnp.int32)
    phase = along[:, None] * waves[None, :] % width
    angle = 2.0 * math.pi / width * phase.astype(jnp.float32)
    factor = 1.0 / math.sqrt(width)
    forward = jnp.concatenate([jnp.cos(angle), -jnp.sin(angle)], axis=1) * factor
    weight_k = jnp.where(waves == 0, 1.0, 2.0).astype(jnp.float32)
    inverse = (
        jnp.concatenate([jnp.cos(angle) * weight_k, -jnp.sin(angle) * weight_k], axis=1).T * factor
    )
    return (forward.astype(jnp.bfloat16), inverse.astype(jnp.bfloat16))


def lat_tables(length):
    index = jnp.arange(length, dtype=jnp.int32)
    phase = index[:, None] * index[None, :] % length
    angle = 2.0 * math.pi / length * phase.astype(jnp.float32)
    factor = 1.0 / math.sqrt(length)
    return (
        (jnp.cos(angle) * factor).astype(jnp.bfloat16),
        (jnp.sin(angle) * factor).astype(jnp.bfloat16),
    )


def layer_norm(values, gain, shift):
    center = jnp.mean(values, axis=-1, keepdims=True)
    spread = jnp.mean(jnp.square(values - center), axis=-1, keepdims=True)
    return (values - center) * lax.rsqrt(spread + 1e-05) * gain + shift


def matmul(left, right):
    return jnp.dot(left, right, preferred_element_type=jnp.float32)


def block_product(left, weight):
    return jnp.einsum("rnb,nbe->rne", left, weight, preferred_element_type=jnp.float32)


def block_mix(part_re, part_im, weight, bias):
    count = part_re.shape[0]
    blocks = weight.shape[1]
    inner = weight.shape[2]
    left_re = part_re.reshape(count, blocks, inner)
    left_im = part_im.reshape(count, blocks, inner)
    out_re = block_product(left_re, weight[0]) - block_product(left_im, weight[1])
    out_im = block_product(left_re, weight[1]) + block_product(left_im, weight[0])
    return (out_re.reshape(count, -1) + bias[0], out_im.reshape(count, -1) + bias[1])


def shrink(values):
    return jnp.sign(values) * jnp.maximum(jnp.abs(values) - 0.01, 0.0)


def filter_group(
    normed_group, forward, inverse, lat_cos, lat_sin, weight_one, bias_one, weight_two, bias_two
):
    chans = normed_group.shape[3]
    kept = forward.shape[1] // 2
    spectrum = jnp.einsum(
        "shwc,wk->hskc", normed_group, forward, preferred_element_type=jnp.float32
    ).astype(jnp.bfloat16)
    a_re = spectrum[:, :, :kept]
    a_im = spectrum[:, :, kept:]
    m_re, m_im = (
        lax.all_to_all(a_re, "lat", split_axis=2, concat_axis=0, tiled=True),
        lax.all_to_all(a_im, "lat", split_axis=2, concat_axis=0, tiled=True),
    )
    lat_len = m_re.shape[0]
    sample_count = m_re.shape[1]
    local_waves = m_re.shape[2]
    flat_re = m_re.reshape(lat_len, sample_count * local_waves * chans)
    flat_im = m_im.reshape(lat_len, sample_count * local_waves * chans)
    b_re = (matmul(lat_cos, flat_re) + matmul(lat_sin, flat_im)).astype(jnp.bfloat16)
    b_im = (matmul(lat_cos, flat_im) - matmul(lat_sin, flat_re)).astype(jnp.bfloat16)
    modes = lat_len * sample_count * local_waves
    first_re, first_im = block_mix(
        b_re.reshape(modes, chans), b_im.reshape(modes, chans), weight_one, bias_one
    )
    first_re = jax.nn.relu(first_re).astype(jnp.bfloat16)
    first_im = jax.nn.relu(first_im).astype(jnp.bfloat16)
    second_re, second_im = block_mix(first_re, first_im, weight_two, bias_two)
    second_re = shrink(second_re).astype(jnp.bfloat16).reshape(lat_len, -1)
    second_im = shrink(second_im).astype(jnp.bfloat16).reshape(lat_len, -1)
    y_re = (matmul(lat_cos, second_re) - matmul(lat_sin, second_im)).astype(jnp.bfloat16)
    y_im = (matmul(lat_cos, second_im) + matmul(lat_sin, second_re)).astype(jnp.bfloat16)
    shaped = (lat_len, sample_count, local_waves, chans)
    back_re, back_im = (
        lax.all_to_all(y_re.reshape(shaped), "lat", split_axis=0, concat_axis=2, tiled=True),
        lax.all_to_all(y_im.reshape(shaped), "lat", split_axis=0, concat_axis=2, tiled=True),
    )
    joined = jnp.concatenate([back_re, back_im], axis=2)
    return jnp.einsum("hskc,kw->shwc", joined, inverse, preferred_element_type=jnp.float32)


def local(
    state_field,
    norm1_gain,
    norm1_shift,
    spec_w1,
    spec_b1,
    spec_w2,
    spec_b2,
    norm2_gain,
    norm2_shift,
    fc1_weight,
    fc1_bias,
    fc2_weight,
    fc2_bias,
):
    sample_count = state_field.shape[0]
    row_count = state_field.shape[1]
    width = state_field.shape[2]
    chans = state_field.shape[3]
    lat_len = row_count * lax.axis_size("lat")
    values = state_field.astype(jnp.float32)
    normed = layer_norm(values, norm1_gain, norm1_shift).astype(jnp.bfloat16)
    forward, inverse = lon_tables(width, KW)
    lat_cos, lat_sin = lat_tables(lat_len)
    filtered_parts = filter_group(
        normed, forward, inverse, lat_cos, lat_sin, spec_w1, spec_b1, spec_w2, spec_b2
    )
    mixed_state = filtered_parts + normed.astype(jnp.float32) + values
    total_rows = sample_count * row_count * width
    second_norm = (
        layer_norm(mixed_state, norm2_gain, norm2_shift)
        .astype(jnp.bfloat16)
        .reshape(total_rows, chans)
    )
    hidden = jax.nn.gelu(matmul(second_norm, fc1_weight) + fc1_bias).astype(jnp.bfloat16)
    result = mixed_state.reshape(total_rows, chans) + matmul(hidden, fc2_weight) + fc2_bias
    return result.astype(jnp.bfloat16).reshape(sample_count, row_count, width, chans)


def solution(mesh):
    return jax.shard_map(
        local,
        mesh=mesh,
        in_specs=(
            P("grp", "lat", None, None),
            P(),
            P(),
            P(),
            P(),
            P(),
            P(),
            P(),
            P(),
            P(),
            P(),
            P(),
            P(),
        ),
        out_specs=P("grp", "lat", None, None),
        check_vma=False,
    )
```

profile of v0, /device:TPU:13, one launch (start us, length us, event | category | flops | bytes accessed | tf_op | source)
XLA Modules:
  0.0 250.9 jit_solution(17199923472469534109)
XLA Ops:
  0.4 2.7 %convert_reduce_fusion = f32[4,3,180]{2,0,1:T(4,128)S(1)} fusion(bf16[4,3,180,768]{3,0,2,1:T(4,128)(2,1)} %param.13), kind=kLoop, calls=%fused_computation.19 | loop fusion | flops 3315600 | bytes 3326400 | tf_op jit(solution)/shard_map/reduce_sum | solution.py:37
  4.5 2.3 convert_bitcast_fusion
  7.0 2.0 copy.71
  8.9 6.6 %all-to-all-start.1 = ((bf16[3,4,64,768]{3,1,0,2:T(4,128)(2,1)}), bf16[3,4,64,768]{3,1,0,2:T(4,128)(2,1)S(1)}, u32[]{:S(2)}, u32[]{:S(2)}) async-start(bf16[3,4,64,768]{3,1,0,2:T(4,128)(2,1)} %copy.71), calls=%async_computation.1 | async-start | bytes 2359296 | tf_op jit(solution)/shard_map/all_to_all | solution.py:77
  17.5 25.8 %all-to-all-done.1 = bf16[3,4,64,768]{3,1,0,2:T(4,128)(2,1)S(1)} async-done(((bf16[3,4,64,768]{3,1,0,2:T(4,128)(2,1)}), bf16[3,4,64,768]{3,1,0,2:T(4,128)(2,1)S(1)}, u32[]{:S(2)}, u32[]{:S(2)}) %all-to-all-start.1) | async-done | bytes 1179680 | tf_op jit(solution)/shard_map/all_to_all | solution.py:77
  43.3 5.1 %all-to-all-start = ((bf16[3,4,64,768]{3,1,0,2:T(4,128)(2,1)}), bf16[3,4,64,768]{3,1,0,2:T(4,128)(2,1)S(1)}, u32[]{:S(2)}, u32[]{:S(2)}) async-start(bf16[3,4,64,768]{3,1,0,2:T(4,128)(2,1)} %copy.69), calls=%async_computation | async-start | bytes 2359296 | tf_op jit(solution)/shard_map/all_to_all | solution.py:76
  53.8 22.2 %all-to-all-done = bf16[3,4,64,768]{3,1,0,2:T(4,128)(2,1)S(1)} async-done(((bf16[3,4,64,768]{3,1,0,2:T(4,128)(2,1)}), bf16[3,4,64,768]{3,1,0,2:T(4,128)(2,1)S(1)}, u32[]{:S(2)}, u32[]{:S(2)}) %all-to-all-start) | async-done | bytes 1179680 | tf_op jit(solution)/shard_map/all_to_all | solution.py:76
  78.6 2.5 reshape_reshape.6
  81.1 2.1 copy.74
  87.9 2.5 reshape_reshape.7
  90.4 2.1 copy.76
  97.9 2.3 copy.81
  100.3 3.2 %reshape.86 = f32[48,12288]{1,0:T(8,128)S(1)} reshape(f32[768,8,96]{2,1,0:T(8,128)} %copy.81) | data formatting | bytes 4718592 | tf_op jit(solution)/shard_map/reshape | solution.py:58
  103.5 3.7 %add_bitcast_fusion = f32[768,8,96]{0,2,1:T(8,128)} fusion(f32[8,768,96]{1,2,0:T(8,128)} %fusion.27, bf16[768,8,96]{0,2,1:T(8,128)(2,1)S(1)} %fusion.26, bf16[2,8,96,96]{3,2,1,0:T(8,128)(2,1)} %param.18), kind=kOutput, calls=%fused_computation.36 | convolution fusion | flops 113836032 | bytes 6094848 | tf_op jit(solution)/shard_map/rnb,nbe->rne/dot_general | solution.py:47
  107.2 3.4 %copy.82 = f32[768,8,96]{2,1,0:T(8,128)} copy(f32[768,8,96]{0,2,1:T(8,128)} %add_bitcast_fusion) | data formatting | bytes 4718592 | tf_op jit(solution)/shard_map/add | solution.py:57
  110.6 4.4 %reshape.87 = f32[48,12288]{1,0:T(8,128)} reshape(f32[768,8,96]{2,1,0:T(8,128)} %copy.82) | data formatting | bytes 4718592 | tf_op jit(solution)/shard_map/reshape | solution.py:58
  120.0 4.9 %all-to-all-start.2 = ((bf16[48,4,4,768]{3,2,1,0:T(4,128)(2,1)}), bf16[48,4,4,768]{3,2,1,0:T(4,128)(2,1)S(1)}, u32[]{:S(2)}, u32[]{:S(2)}) async-start(bf16[48,4,4,768]{3,2,1,0:T(4,128)(2,1)} %reshape.88), calls=%async_computation.2 | async-start | bytes 2359296 | tf_op jit(solution)/shard_map/all_to_all | solution.py:99
  124.9 3.1 %fusion.66 = f32[48,12288]{1,0:T(8,128)S(1)} fusion(f32[48,12288]{1,0:T(8,128)} %reshape.87, f32[12288]{0:T(1024)} %add.194), kind=kOutput, calls=%fused_computation.98 | convolution fusion | flops 60777216 | bytes 4767744 | tf_op jit(solution)/shard_map/dot_general | solution.py:43
  128.0 2.5 %fusion.11 = bf16[48,12288]{1,0:T(8,128)(2,1)} fusion(f32[48,12288]{1,0:T(8,128)S(1)} %fusion.66, f32[48,12288]{1,0:T(8,128)S(1)} %reshape.86, f32[12288]{0:T(1024)S(1)} %copy-done.12), kind=kOutput, calls=%fused_computation.16 | convolution fusion | flops 61956864 | bytes 5947392 | tf_op jit(solution)/shard_map/dot_general | solution.py:43
  130.5 2.8 %reshape.89 = bf16[48,4,4,768]{3,2,1,0:T(4,128)(2,1)} reshape(bf16[48,12288]{1,0:T(8,128)(2,1)} %fusion.11) | data formatting | bytes 2359296 | tf_op jit(solution)/shard_map/reshape | solution.py:100
  133.3 19.3 %all-to-all-done.2 = bf16[48,4,4,768]{3,2,1,0:T(4,128)(2,1)S(1)} async-done(((bf16[48,4,4,768]{3,2,1,0:T(4,128)(2,1)}), bf16[48,4,4,768]{3,2,1,0:T(4,128)(2,1)S(1)}, u32[]{:S(2)}, u32[]{:S(2)}) %all-to-all-start.2) | async-done | bytes 1179680 | tf_op jit(solution)/shard_map/all_to_all | solution.py:99
  152.6 4.9 %all-to-all-start.3 = ((bf16[48,4,4,768]{3,2,1,0:T(4,128)(2,1)}), bf16[48,4,4,768]{3,2,1,0:T(4,128)(2,1)S(1)}, u32[]{:S(2)}, u32[]{:S(2)}) async-start(bf16[48,4,4,768]{3,2,1,0:T(4,128)(2,1)} %reshape.89), calls=%async_computation.3 | async-start | bytes 2359296 | tf_op jit(solution)/shard_map/all_to_all | solution.py:100
  160.3 24.9 %all-to-all-done.3 = bf16[48,4,4,768]{3,2,1,0:T(4,128)(2,1)S(1)} async-done(((bf16[48,4,4,768]{3,2,1,0:T(4,128)(2,1)}), bf16[48,4,4,768]{3,2,1,0:T(4,128)(2,1)S(1)}, u32[]{:S(2)}, u32[]{:S(2)}) %all-to-all-start.3) | async-done | bytes 1179680 | tf_op jit(solution)/shard_map/all_to_all | solution.py:100
  186.3 2.9 %copy.110 = bf16[16,3,4,4,768]{4,3,0,2,1:T(4,128)(2,1)} copy(bf16[16,3,4,4,768]{4,3,2,1,0:T(4,128)(2,1)} %bitcast.97) | data formatting | bytes 2359296 | tf_op jit(solution)/shard_map/all_to_all | solution.py:100
  189.2 3.2 %all_to_all.61 = bf16[3,4,64,768]{3,2,1,0:T(8,128)(2,1)} reshape(bf16[3,4,16,4,768]{4,3,2,1,0:T(4,128)(2,1)} %bitcast.101) | data formatting | bytes 2359296 | tf_op jit(solution)/shard_map/all_to_all | solution.py:100
  192.4 4.4 %fusion.108 = (f32[4,3,180]{2,0,1:T(4,128)S(1)}, f32[4,3,180,768]{3,2,0,1:T(8,128)S(1)}) fusion(f32[768]{0:T(1024)S(1)} %copy-done.24, f32[768]{0:T(1024)S(1)} %copy-done.26, f32[4,3,180]{2,0,1:T(4,128)S(1)} %copy-done.17, f32[4,3,180]{2,0,1:T(4,128)S(1)} %broadcast_multiply_fusion.3, bf16[4,3,180,768]{3,0,2,1:T(4,128)(2,1)S(1)} %copy-done.2, ...), kind=kOutput, calls=%fused_computation.147 | convolution fusion | flops 446047616 | bytes 12436800 | tf_op jit(solution)/shard_map/hskc,kw->shwc/dot_general | solution.py:103
  196.9 3.3 %copy.85 = f32[4,3,180,768]{3,2,1,0:T(8,128)} copy(f32[4,3,180,768]{3,2,0,1:T(8,128)S(1)} %get-tuple-element.14) | data formatting | bytes 13271040 | tf_op jit(solution)/shard_map/add | solution.py:133
  202.6 2.9 %reshape.91 = bf16[2160,768]{1,0:T(8,128)(2,1)} reshape(bf16[4,3,180,768]{3,2,1,0:T(8,128)(2,1)S(1)} %copy.86) | data formatting | bytes 6635520 | tf_op jit(solution)/shard_map/reshape | solution.py:138
  205.5 7.6 %reshape.90 = f32[2160,768]{1,0:T(8,128)} reshape(f32[4,3,180,768]{3,2,1,0:T(8,128)} %copy.85) | data formatting | bytes 13271040 | tf_op jit(solution)/shard_map/reshape | solution.py:141
  213.1 30.6 %add_convert_fusion.1 = bf16[2160,768]{1,0:T(8,128)(2,1)} fusion(f32[2160,768]{1,0:T(8,128)} %reshape.90, bf16[3072,768]{1,0:T(8,128)(2,1)} %param.24, f32[768]{0:T(1024)S(1)} %copy-done.27, bf16[2160,768]{1,0:T(8,128)(2,1)S(1)} %copy-done.7, bf16[768,3072]{1,0:T(8,128)(2,1)} %param.22, f32[3072]{0:T(1024)S(1)} %copy-done.22), kind=kOutput, calls=%fused_computation.29 | convolution fusion | flops 20455649280 | bytes 22723584 | tf_op jit(solution)/shard_map/dot_general | solution.py:43
  243.7 3.7 %reshape.92 = bf16[4,3,180,768]{3,2,1,0:T(8,128)(2,1)S(1)} reshape(bf16[2160,768]{1,0:T(8,128)(2,1)} %add_convert_fusion.1) | data formatting | bytes 6635520 | tf_op jit(solution)/shard_map/reshape | solution.py:142
  247.4 3.0 %copy.87 = bf16[4,3,180,768]{3,0,2,1:T(4,128)(2,1)} copy(bf16[4,3,180,768]{3,2,1,0:T(8,128)(2,1)S(1)} %reshape.92) | data formatting | bytes 6635520 | tf_op jit(solution)/shard_map/reshape | solution.py:142
  (97 shorter events, 33.1 us)
Async XLA Ops:
  0.0 3.1 %copy-start.1 = (bf16[4,3,180,768]{3,0,2,1:T(4,128)(2,1)S(1)}, bf16[4,3,180,768]{3,0,2,1:T(4,128)(2,1)}, u32[]{:S(2)}) copy-start(bf16[4,3,180,768]{3,0,2,1:T(4,128)(2,1)} %param.13) | copy-start | bytes 9953284
  3.1 1.4 copy-start.23
  3.1 1.4 copy-start.25
  4.5 2.3 copy-start.16
  8.9 34.3 %all-to-all-start.1 = ((bf16[3,4,64,768]{3,1,0,2:T(4,128)(2,1)}), bf16[3,4,64,768]{3,1,0,2:T(4,128)(2,1)S(1)}, u32[]{:S(2)}, u32[]{:S(2)}) async-start(bf16[3,4,64,768]{3,1,0,2:T(4,128)(2,1)} %copy.71), calls=%async_computation.1 | async-start | bytes 2359296 | tf_op jit(solution)/shard_map/all_to_all | solution.py:77
  15.5 32.9 %copy-start.18 = (f32[2,768]{1,0:T(2,128)S(1)}, f32[2,768]{1,0:T(2,128)}, u32[]{:S(2)}) copy-start(f32[2,768]{1,0:T(2,128)} %param.17) | copy-start | bytes 18436
  15.5 33.7 %copy-start.19 = (f32[2,768]{1,0:T(2,128)S(1)}, f32[2,768]{1,0:T(2,128)}, u32[]{:S(2)}) copy-start(f32[2,768]{1,0:T(2,128)} %param.19) | copy-start | bytes 18436
  43.3 32.8 %all-to-all-start = ((bf16[3,4,64,768]{3,1,0,2:T(4,128)(2,1)}), bf16[3,4,64,768]{3,1,0,2:T(4,128)(2,1)S(1)}, u32[]{:S(2)}, u32[]{:S(2)}) async-start(bf16[3,4,64,768]{3,1,0,2:T(4,128)(2,1)} %copy.69), calls=%async_computation | async-start | bytes 2359296 | tf_op jit(solution)/shard_map/all_to_all | solution.py:76
  81.1 2.1 copy-start.8
  85.2 2.1 copy-start.3
  87.9 4.6 %copy-start.5 = (f32[8,768,96]{1,2,0:T(8,128)S(1)}, f32[8,768,96]{1,2,0:T(8,128)}, u32[]{:S(2)}) copy-start(f32[8,768,96]{1,2,0:T(8,128)} %fusion.37) | copy-start | bytes 7077892
  92.4 1.5 copy-start.10
  94.5 2.0 copy-start.4
  94.5 2.4 copy-start.9
  110.6 4.5 %copy-start.11 = (f32[12288]{0:T(1024)S(1)}, f32[12288]{0:T(1024)}, u32[]{:S(2)}) copy-start(f32[12288]{0:T(1024)} %add.187) | copy-start | bytes 147460
  115.1 1.7 copy-start
  115.1 1.7 copy-start.13
  120.0 32.6 %all-to-all-start.2 = ((bf16[48,4,4,768]{3,2,1,0:T(4,128)(2,1)}), bf16[48,4,4,768]{3,2,1,0:T(4,128)(2,1)S(1)}, u32[]{:S(2)}, u32[]{:S(2)}) async-start(bf16[48,4,4,768]{3,2,1,0:T(4,128)(2,1)} %reshape.88), calls=%async_computation.2 | async-start | bytes 2359296 | tf_op jit(solution)/shard_map/all_to_all | solution.py:99
  124.9 3.1 %copy-start.12 = (f32[12288]{0:T(1024)S(1)}, f32[12288]{0:T(1024)}, u32[]{:S(2)}) copy-start(f32[12288]{0:T(1024)} %add.187) | copy-start | bytes 147460
  152.6 32.6 %all-to-all-start.3 = ((bf16[48,4,4,768]{3,2,1,0:T(4,128)(2,1)}), bf16[48,4,4,768]{3,2,1,0:T(4,128)(2,1)S(1)}, u32[]{:S(2)}, u32[]{:S(2)}) async-start(bf16[48,4,4,768]{3,2,1,0:T(4,128)(2,1)} %reshape.89), calls=%async_computation.3 | async-start | bytes 2359296 | tf_op jit(solution)/shard_map/all_to_all | solution.py:100
  185.3 1.0 copy-start.6
  186.3 6.1 %copy-start.2 = (bf16[4,3,180,768]{3,0,2,1:T(4,128)(2,1)S(1)}, bf16[4,3,180,768]{3,0,2,1:T(4,128)(2,1)}, u32[]{:S(2)}) copy-start(bf16[4,3,180,768]{3,0,2,1:T(4,128)(2,1)} %param.13) | copy-start | bytes 9953284
  186.3 6.1 %copy-start.14 = (f32[180,64]{1,0:T(8,128)S(1)}, f32[180,64]{1,0:T(8,128)}, u32[]{:S(2)}) copy-start(f32[180,64]{1,0:T(8,128)} %get-tuple-element.11) | copy-start | bytes 138244
  186.3 6.1 %copy-start.15 = (f32[180,64]{1,0:T(8,128)S(1)}, f32[180,64]{1,0:T(8,128)}, u32[]{:S(2)}) copy-start(f32[180,64]{1,0:T(8,128)} %get-tuple-element.12) | copy-start | bytes 138244
  186.3 6.1 %copy-start.17 = (f32[4,3,180]{2,0,1:T(4,128)S(1)}, f32[4,3,180]{2,0,1:T(4,128)}, u32[]{:S(2)}) copy-start(f32[4,3,180]{2,0,1:T(4,128)} %copy-done.16) | copy-start | bytes 25924
  186.3 6.2 %copy-start.24 = (f32[768]{0:T(1024)S(1)}, f32[768]{0:T(1024)}, u32[]{:S(2)}) copy-start(f32[768]{0:T(1024)} %param.15) | copy-start | bytes 9220
  186.3 6.1 %copy-start.26 = (f32[768]{0:T(1024)S(1)}, f32[768]{0:T(1024)}, u32[]{:S(2)}) copy-start(f32[768]{0:T(1024)} %param.14) | copy-start | bytes 9220
  200.1 0.9 copy-start.20
  200.1 1.0 copy-start.21
  205.5 7.6 %copy-start.7 = (bf16[2160,768]{1,0:T(8,128)(2,1)S(1)}, bf16[2160,768]{1,0:T(8,128)(2,1)}, u32[]{:S(2)}) copy-start(bf16[2160,768]{1,0:T(8,128)(2,1)} %reshape.91) | copy-start | bytes 9953284
  205.5 7.6 %copy-start.22 = (f32[3072]{0:T(1024)S(1)}, f32[3072]{0:T(1024)}, u32[]{:S(2)}) copy-start(f32[3072]{0:T(1024)} %param.23) | copy-start | bytes 36868
  205.5 7.6 %copy-start.27 = (f32[768]{0:T(1024)S(1)}, f32[768]{0:T(1024)}, u32[]{:S(2)}) copy-start(f32[768]{0:T(1024)} %param.25) | copy-start | bytes 9220
where the time goes:
time: 256 us; the launch traced here: 251 us
  waiting for transfers between devices  92.3 us (36%)
  local copies, waits for them, and re-layouts  66.3 us (26%)
  matrix products  62.2 us (24%)
  starting transfers between devices  21.4 us (8%)
  other arithmetic  7.73 us (3%)
    dot_general x9, matrix products, matmul(): return jnp.dot(left, right, preferred_element_type=jnp.float32)  42.9 us
    all_to_all x1, waiting for transfers between devices, filter_group(): lax.all_to_all(a_im, 'lat', split_axis=2, concat_axis=0, tiled=True)  25.8 us
    all_to_all x1, waiting for transfers between devices, filter_group(): lax.all_to_all(y_im.reshape(shaped), 'lat', split_axis=0, concat_axis=2,...  24.9 us
    all_to_all x1, waiting for transfers between devices, filter_group(): lax.all_to_all(a_re, 'lat', split_axis=2, concat_axis=0, tiled=True)  22.2 us
    all_to_all x1, waiting for transfers between devices, filter_group(): lax.all_to_all(y_re.reshape(shaped), 'lat', split_axis=0, concat_axis=2,...  19.3 us
    dot_general x8, matrix products, block_product(): jnp.einsum('rnb,nbe->rne', left, weight, preferred_element_type=jnp.float32)  12.6 us
    reshape x1, local copies, waits for them, and re-layouts, local(): mixed_state.reshape(total_rows, chans) + matmul(hidden, fc2_weight)  7.57 us
    reshape x2, local copies, waits for them, and re-layouts, local(): result.astype(jnp.bfloat16).reshape(sample_count, row_count, width, chans)  6.75 us
  transfers between devices with their start and end apart: 4, of which 4 were waited for; matrix products, arithmetic and copies ran while one was open for 7% of the time, Pallas kernels for 0%

commit v1 on v0

v1 whole, which is shorter than its diff:
```python
import functools
import math

import jax
import jax.numpy as jnp
import numpy as np
from jax import lax
from jax.experimental import pallas as pl
from jax.experimental.pallas import tpu as pltpu
from jax.sharding import PartitionSpec as P

KW = 64
BF = jnp.bfloat16
F32 = jnp.float32
FIRST_CHUNKS = (2, 2)
SECOND_CHUNKS = (2, 2)


def lon_tables(width, kept, chips):
    along = np.arange(width)
    waves = np.arange(kept)
    angle = 2.0 * math.pi / width * (along[:, None] * waves[None, :] % width)
    factor = 1.0 / math.sqrt(width)
    weight_k = np.where(waves == 0, 1.0, 2.0)
    split = (width, chips, kept // chips)
    forward = np.stack(
        [np.cos(angle).reshape(split), -np.sin(angle).reshape(split)], axis=2
    ).reshape(width, 2 * kept)
    inverse = np.stack(
        [(np.cos(angle) * weight_k).reshape(split), (-np.sin(angle) * weight_k).reshape(split)],
        axis=2,
    ).reshape(width, 2 * kept)
    to_bf = lambda t: jnp.asarray((t * factor).astype(np.float32).astype(jnp.bfloat16))
    return to_bf(forward.T), to_bf(inverse)


def lat_tables(length, waves):
    index = np.arange(length)
    angle = 2.0 * math.pi / length * (index[:, None] * index[None, :] % length)
    cos = np.cos(angle) / math.sqrt(length)
    sin = np.sin(angle) / math.sqrt(length)
    eye = np.eye(waves)
    parts = np.array([[cos, sin], [-sin, cos]])
    size = 2 * length * waves
    forward = np.einsum("pqmh,kl->pmkhql", parts, eye).reshape(size, size)
    parts = np.array([[cos, -sin], [sin, cos]])
    inverse = np.einsum("pqhm,kl->hpkqml", parts, eye).reshape(size, size)
    to_bf = lambda t: jnp.asarray(t.astype(np.float32).astype(jnp.bfloat16))
    return to_bf(forward), to_bf(inverse)


def normalize(values, gain, shift):
    center = jnp.mean(values, axis=-1, keepdims=True)
    away = values - center
    spread = jnp.mean(away * away, axis=-1, keepdims=True)
    return away * lax.rsqrt(spread + 1e-05) * gain + shift


def dot(left, right):
    return jnp.dot(left, right, preferred_element_type=F32)


def forward_kernel(place, x_ref, gain, shift, table, own_ref, other_ref, spec):
    chips = own_ref.shape[0]
    half = own_ref.shape[3]
    rows = x_ref.shape[1]
    span = own_ref.shape[2] // rows
    chip = place[0] // 2
    core = place[0] % 2
    for r in range(rows):
        normed = normalize(x_ref[0, r].astype(F32), gain[...], shift[...]).astype(BF)
        spec[r] = dot(table[...], normed)
    near = pl.ds(pl.multiple_of(core * half, 128), half)
    far = pl.ds(pl.multiple_of((1 - core) * half, 128), half)
    for m in range(chips):
        source = pl.ds(pl.multiple_of((chip ^ m) * span, 8), span)
        for r in range(rows):
            own_ref[m, 0, r * span : (r + 1) * span, :] = spec[r, source, near].astype(BF)
            other_ref[m, 0, r * span : (r + 1) * span, :] = spec[r, source, far].astype(BF)


def forward_part(place, state, gain, shift, table, start, count, chips):
    rows, width, chans = state.shape[1:]
    block = rows * (table.shape[0] // chips)
    half = chans // 2
    out = jax.ShapeDtypeStruct((chips, count, block, half), BF)
    out_spec = pl.BlockSpec((chips, 1, block, half), lambda s, p: (0, s, 0, 0))
    whole = lambda s, p: (0, 0)
    return pl.pallas_call(
        forward_kernel,
        grid_spec=pltpu.PrefetchScalarGridSpec(
            num_scalar_prefetch=1,
            grid=(count,),
            in_specs=[
                pl.BlockSpec((1, rows, width, chans), lambda s, p: (s + start, 0, 0, 0)),
                pl.BlockSpec((1, chans), whole),
                pl.BlockSpec((1, chans), whole),
                pl.BlockSpec(table.shape, whole),
            ],
            out_specs=[out_spec, out_spec],
            scratch_shapes=[pltpu.VMEM((rows, table.shape[0], chans), F32)],
        ),
        out_shape=[out, out],
        compiler_params=pltpu.CompilerParams(vmem_limit_bytes=24 * 2**20),
        cost_estimate=pl.CostEstimate(
            flops=2 * count * rows * width * chans * table.shape[0],
            bytes_accessed=2 * count * rows * width * chans * 2,
            transcendentals=0,
        ),
        name="lon_forward",
    )(place, state, gain, shift, table)


def mix_kernel(chips, place, *refs):
    parts = refs[:chips]
    lat_in, w_one, b_one, w_two, b_two, lat_out = refs[chips : chips + 6]
    own_ref, other_ref, gathered, spread = refs[chips + 6 :]
    block = own_ref.shape[2]
    half = own_ref.shape[3]
    size = lat_in.shape[0]
    me = place[0]
    for m in range(chips):
        for e in range(2):
            where = pl.ds(pl.multiple_of((me ^ (2 * m + e)) * block, 8), block)
            gathered[where, :] = parts[m][0, e].astype(gathered.dtype)
    modes = dot(lat_in[...], gathered[...].astype(BF)).astype(BF)
    modes = jnp.concatenate([modes[: size // 2], modes[size // 2 :]], axis=1)
    first = jnp.maximum(dot(modes, w_one[...]) + b_one[...], 0.0).astype(BF)
    second = dot(first, w_two[...]) + b_two[...]
    second = second - jnp.clip(second, -0.01, 0.01)
    second = second.astype(BF)
    second = jnp.concatenate([second[:, :half], second[:, half:]], axis=0)
    spread[...] = dot(lat_out[...], second).astype(spread.dtype)
    for m in range(chips):
        for e, out_ref in enumerate((own_ref, other_ref)):
            where = pl.ds(pl.multiple_of((me ^ (2 * m + e)) * block, 8), block)
            out_ref[m, 0] = spread[where, :].astype(BF)


def mix_part(place, parts, lat_in, w_one, b_one, w_two, b_two, lat_out):
    chips = len(parts)
    count, pair, block, half = parts[0].shape
    size = lat_in.shape[0]
    kind = BF if block % 16 == 0 else F32
    out = jax.ShapeDtypeStruct((chips, count, block, half), BF)
    out_spec = pl.BlockSpec((chips, 1, block, half), lambda s, p: (0, s, 0, 0))
    whole = lambda s, p: (0, 0)
    table = lambda t: pl.BlockSpec(t.shape, whole)
    return pl.pallas_call(
        functools.partial(mix_kernel, chips),
        grid_spec=pltpu.PrefetchScalarGridSpec(
            num_scalar_prefetch=1,
            grid=(count,),
            in_specs=[pl.BlockSpec((1, pair, block, half), lambda s, p: (s, 0, 0, 0))] * chips
            + [table(t) for t in (lat_in, w_one, b_one, w_two, b_two, lat_out)],
            out_specs=[out_spec, out_spec],
            scratch_shapes=[pltpu.VMEM((size, half), kind), pltpu.VMEM((size, half), kind)],
        ),
        out_shape=[out, out],
        compiler_params=pltpu.CompilerParams(vmem_limit_bytes=32 * 2**20),
        cost_estimate=pl.CostEstimate(
            flops=4 * count * (size * size * half + size // 2 * 4 * half * half),
            bytes_accessed=4 * count * size * half * 2,
            transcendentals=0,
        ),
        name="mix_modes",
    )(place, *parts, lat_in, w_one, b_one, w_two, b_two, lat_out)


def final_kernel(chips, place, *refs):
    parts = refs[:chips]
    x_ref, gain1, shift1, table, gain2, shift2, fc1, bias1, fc2, bias2 = refs[chips : chips + 10]
    out_ref, spec, mixed, act, total = refs[-5:]
    rows = x_ref.shape[1]
    width = x_ref.shape[2]
    half = parts[0].shape[3]
    span = parts[0].shape[2] // rows
    pitch = mixed.shape[0] // rows
    chip = place[0] // 2
    core = place[0] % 2
    near = pl.ds(pl.multiple_of(core * half, 128), half)
    far = pl.ds(pl.multiple_of((1 - core) * half, 128), half)
    for m in range(chips):
        where = pl.ds(pl.multiple_of((chip ^ m) * span, 8), span)
        for r in range(rows):
            cut = slice(r * span, (r + 1) * span)
            spec[r, where, near] = parts[m][0, 0, cut, :].astype(spec.dtype)
            spec[r, where, far] = parts[m][0, 1, cut, :].astype(spec.dtype)
    for r in range(rows):
        values = x_ref[0, r].astype(F32)
        normed = normalize(values, gain1[...], shift1[...]).astype(BF).astype(F32)
        state = dot(table[...], spec[r].astype(BF)) + normed + values
        mixed[r * pitch : r * pitch + width, :] = state
        act[r * pitch : r * pitch + width, :] = normalize(state, gain2[...], shift2[...]).astype(BF)
    hidden = fc1.shape[1]
    step = hidden // 4
    normed2 = act[...]
    for f in range(4):
        cut = slice(f * step, (f + 1) * step)
        inner = dot(normed2, fc1[:, cut]) + bias1[:, cut]
        inner = jax.nn.gelu(inner).astype(BF)
        piece = dot(inner, fc2[cut, :])
        if f == 0:
            total[...] = piece
        else:
            total[...] += piece
    for r in range(rows):
        cut = slice(r * pitch, r * pitch + width)
        out_ref[0, r] = (mixed[cut, :] + total[cut, :] + bias2[...]).astype(BF)


def final_part(place, parts, state, vectors1, table, vectors2, fc1, bias1, fc2, bias2, start, so_far):
    chips = len(parts)
    count, pair, block, half = parts[0].shape
    rows, width, chans = state.shape[1:]
    span = block // rows
    pitch = (width + 15) // 16 * 16
    kind = BF if span % 16 == 0 else F32
    whole = lambda s, p: (0, 0)
    table_spec = lambda t: pl.BlockSpec(t.shape, whole)
    token_spec = pl.BlockSpec((1, rows, width, chans), lambda s, p: (s + start, 0, 0, 0))
    operands = [state, *vectors1, table, *vectors2, fc1, bias1, fc2, bias2]
    in_specs = [pl.BlockSpec((1, pair, block, half), lambda s, p: (s, 0, 0, 0))] * chips
    in_specs += [token_spec] + [table_spec(t) for t in operands[1:]]
    aliases = {}
    if so_far is not None:
        aliases = {1 + len(in_specs): 0}
        in_specs += [pl.BlockSpec(memory_space=pl.ANY)]
        operands.append(so_far)
    return pl.pallas_call(
        functools.partial(final_kernel, chips),
        grid_spec=pltpu.PrefetchScalarGridSpec(
            num_scalar_prefetch=1,
            grid=(count,),
            in_specs=in_specs,
            out_specs=token_spec,
            scratch_shapes=[
                pltpu.VMEM((rows, chips * span, chans), kind),
                pltpu.VMEM((rows * pitch, chans), F32),
                pltpu.VMEM((rows * pitch, chans), BF),
                pltpu.VMEM((rows * pitch, chans), F32),
            ],
        ),
        out_shape=jax.ShapeDtypeStruct(state.shape, BF),
        input_output_aliases=aliases,
        compiler_params=pltpu.CompilerParams(vmem_limit_bytes=48 * 2**20),
        cost_estimate=pl.CostEstimate(
            flops=4 * count * rows * width * chans * fc1.shape[1],
            bytes_accessed=4 * count * rows * width * chans + 4 * chans * fc1.shape[1],
            transcendentals=count * rows * width * fc1.shape[1],
        ),
        name="channel_mlp",
    )(place, *parts, *operands)


def mixing_weights(weight, bias, core):
    blocks = weight.shape[1] // 2
    inner = weight.shape[2]
    half = blocks * inner
    own = lax.dynamic_slice_in_dim(weight, core * blocks, blocks, 1)
    eye = jnp.eye(blocks, dtype=weight.dtype)
    wide = (own[:, :, :, None, :] * eye[None, :, None, :, None]).reshape(2, half, half)
    matrix = jnp.concatenate(
        [
            jnp.concatenate([wide[0], wide[1]], axis=1),
            jnp.concatenate([-wide[1], wide[0]], axis=1),
        ],
        axis=0,
    )
    return matrix, lax.dynamic_slice_in_dim(bias, core * half, half, 1).reshape(1, 2 * half)


def swap_cores(array, devices):
    return lax.ppermute(array, "lat", [(i, i ^ 1) for i in range(devices)])


def swap_chips(own, other, devices):
    parts = []
    for m in range(own.shape[0]):
        part = jnp.stack([own[m], other[m]], axis=1)
        if m > 0:
            part = lax.ppermute(part, "lat", [(i, i ^ (2 * m)) for i in range(devices)])
        parts.append(part)
    return parts


def local(devices, *args):
    (state, gain1, shift1, w_one, b_one, w_two, b_two, gain2, shift2, fc1, bias1, fc2, bias2) = args
    samples, rows, width, chans = state.shape
    chips = devices // 2
    me = lax.axis_index("lat")
    place = me.astype(jnp.int32).reshape(1)
    core = me % 2
    row = lambda v: v.reshape(1, -1)
    forward, inverse = lon_tables(width, KW, chips)
    lat_in, lat_out = lat_tables(rows * devices, KW // chips)
    mix_one = mixing_weights(w_one, b_one, core)
    mix_two = mixing_weights(w_two, b_two, core)

    middle = []
    start = 0
    for count in FIRST_CHUNKS:
        own, other = forward_part(
            place, state, row(gain1), row(shift1), forward, start, count, chips
        )
        parts = swap_chips(own, swap_cores(other, devices), devices)
        middle.append(mix_part(place, parts, lat_in, *mix_one, *mix_two, lat_out))
        start += count

    result = None
    start = 0
    for (own, other), count in zip(middle, SECOND_CHUNKS):
        parts = swap_chips(own, swap_cores(other, devices), devices)
        result = final_part(
            place,
            parts,
            state,
            (row(gain1), row(shift1)),
            inverse,
            (row(gain2), row(shift2)),
            fc1,
            row(bias1),
            fc2,
            row(bias2),
            start,
            result,
        )
        start += count
    return result


def solution(mesh):
    tokens = P("grp", "lat", None, None)
    return jax.shard_map(
        functools.partial(local, mesh.shape["lat"]),
        mesh=mesh,
        in_specs=(tokens,) + (P(),) * 12,
        out_specs=tokens,
        check_vma=False,
    )
```

time: 256 us -> 169 us (0.66)
  the two profiles are of different devices: /device:TPU:13 before, /device:TPU:0 now
where the time goes in v1:
time: 169 us
  starting transfers between devices  89.5 us (53%)
  Pallas kernels  53.3 us (32%)
  local copies, waits for them, and re-layouts  14.2 us (8%)
  waiting for transfers between devices  9.19 us (5%)
  other arithmetic  1.84 us (1%)
    ppermute x28, starting transfers between devices, swap_chips(): part = lax.ppermute(part, 'lat', [(i, i ^ 2 * m) for i in range(devices)])  88.2 us
    pallas_call x2, Pallas kernels, final_part(): pl.pallas_call(functools.partial(final_kernel, chips), grid_spec=pltpu.Pr...  37.4 us
    pallas_call x2, Pallas kernels, mix_part(): pl.pallas_call(functools.partial(mix_kernel, chips), grid_spec=pltpu.Pref...  10.8 us
    ppermute x28, waiting for transfers between devices, swap_chips(): part = lax.ppermute(part, 'lat', [(i, i ^ 2 * m) for i in range(devices)])  9.18 us
    pallas_call x2, Pallas kernels, forward_part(): pl.pallas_call(forward_kernel, grid_spec=pltpu.PrefetchScalarGridSpec(num...  5.18 us
    unnamed x38, local copies, waits for them, and re-layouts  4.99 us
  transfers between devices with their start and end apart: 32, of which 5 were waited for; matrix products, arithmetic and copies ran while one was open for 4% of the time, Pallas kernels for 19%

profile of v1, /device:TPU:0, one launch (start us, length us, event | category | flops | bytes accessed | tf_op | source)
XLA Modules:
  0.0 169.0 jit_solution(5400169715610040083)
XLA Ops:
  1.4 2.4 %copy.19.x_ref.refs_8_ = bf16[4,3,180,768]{3,2,1,0:T(8,128)(2,1)S(1)} copy(bf16[4,3,180,768]{3,0,2,1:T(4,128)(2,1)} %param.17) | data formatting | bytes 6635520 | tf_op args[0]
  3.8 2.6 %lon_forward.3 = (bf16[8,2,48,384]{3,2,1,0:T(8,128)(2,1)S(1)}, bf16[8,2,48,384]{3,2,1,0:T(8,128)(2,1)}) custom-call(s32[1]{0:T(128)} %bitcast.place, bf16[4,3,180,768]{3,2,1,0:T(8,128)(2,1)S(1)} %copy.19.x_ref.refs_8_, f32[1,768]{1,0:T(1,128)S(1)} %reshape.58.gain.refs_9_, f32[1,768]{1,0:T(1,128)S(1)} %reshape.59.shift.refs_10_, bf16[128,180]{1,0:T(8,128)(2,1)S(1)} %copy-done.5), custom_call_target="tpu_custom_call" | custom-call | flops 212336640 | bytes 3317760 | tf_op jit(solution)/shard_map/lon_forward/pallas_call | solution.py:89
  7.8 2.6 %lon_forward.2 = (bf16[8,2,48,384]{3,2,1,0:T(8,128)(2,1)S(1)}, bf16[8,2,48,384]{3,2,1,0:T(8,128)(2,1)}) custom-call(s32[1]{0:T(128)} %bitcast.place, bf16[4,3,180,768]{3,2,1,0:T(8,128)(2,1)S(1)} %copy.19.x_ref.refs_8_, f32[1,768]{1,0:T(1,128)S(1)} %reshape.58.gain.refs_9_, f32[1,768]{1,0:T(1,128)S(1)} %reshape.59.shift.refs_10_, bf16[128,180]{1,0:T(8,128)(2,1)S(1)} %copy-done.5), custom_call_target="tpu_custom_call" | custom-call | flops 212336640 | bytes 3317760 | tf_op jit(solution)/shard_map/lon_forward/pallas_call | solution.py:89
  15.3 1.2 slice_bitcast_fusion.8
  16.6 3.0 %collective-permute-start.17 = (bf16[2,2,48,384]{3,2,0,1:T(8,128)(2,1)S(1)}, bf16[2,2,48,384]{3,2,0,1:T(8,128)(2,1)S(1)}, u32[]{:S(2)}, u32[]{:S(2)}) collective-permute-start(bf16[2,2,48,384]{3,2,0,1:T(8,128)(2,1)S(1)} %pad_maximum_fusion.17), channel_id=1, source_target_pairs={{0,2},{1,3},{2,0},{3,1},{4,6},{5,7},{6,4},{7,5},{8,10},{9,11},{10,... | collective-permute-start | bytes 442376 | tf_op jit(solution)/shard_map/ppermute | solution.py:282
  19.6 1.6 collective-permute-start.18
  21.4 3.0 %collective-permute-start.20 = (bf16[2,2,48,384]{3,2,0,1:T(8,128)(2,1)S(1)}, bf16[2,2,48,384]{3,2,0,1:T(8,128)(2,1)S(1)}, u32[]{:S(2)}, u32[]{:S(2)}) collective-permute-start(bf16[2,2,48,384]{3,2,0,1:T(8,128)(2,1)S(1)} %pad_maximum_fusion.20), channel_id=1, source_target_pairs={{0,8},{1,9},{2,10},{3,11},{4,12},{5,13},{6,14},{7,15},{8,0},{9,1},... | collective-permute-start | bytes 442376 | tf_op jit(solution)/shard_map/ppermute | solution.py:282
  24.5 1.4 collective-permute-start.21
  25.9 1.2 slice_bitcast_fusion.24
  27.3 3.7 %collective-permute-start.22 = (bf16[2,2,48,384]{3,2,0,1:T(8,128)(2,1)S(1)}, bf16[2,2,48,384]{3,2,0,1:T(8,128)(2,1)S(1)}, u32[]{:S(2)}, u32[]{:S(2)}) collective-permute-start(bf16[2,2,48,384]{3,2,0,1:T(8,128)(2,1)S(1)} %pad_maximum_fusion.22), channel_id=1, source_target_pairs={{0,12},{1,13},{2,14},{3,15},{4,8},{5,9},{6,10},{7,11},{8,4},{9,5},... | collective-permute-start | bytes 442376 | tf_op jit(solution)/shard_map/ppermute | solution.py:282
  32.8 2.3 %collective-permute-start.1 = (bf16[2,2,48,384]{3,2,0,1:T(8,128)(2,1)S(1)}, bf16[2,2,48,384]{3,2,0,1:T(8,128)(2,1)S(1)}, u32[]{:S(2)}, u32[]{:S(2)}) collective-permute-start(bf16[2,2,48,384]{3,2,0,1:T(8,128)(2,1)S(1)} %pad_maximum_fusion.1), channel_id=1, source_target_pairs={{0,2},{1,3},{2,0},{3,1},{4,6},{5,7},{6,4},{7,5},{8,10},{9,11},{10,... | collective-permute-start | bytes 442376 | tf_op jit(solution)/shard_map/ppermute | solution.py:282
  35.2 7.4 %collective-permute-start.2 = (bf16[2,2,48,384]{3,2,0,1:T(8,128)(2,1)S(1)}, bf16[2,2,48,384]{3,2,0,1:T(8,128)(2,1)S(1)}, u32[]{:S(2)}, u32[]{:S(2)}) collective-permute-start(bf16[2,2,48,384]{3,2,0,1:T(8,128)(2,1)S(1)} %pad_maximum_fusion.2), channel_id=1, source_target_pairs={{0,4},{1,5},{2,6},{3,7},{4,0},{5,1},{6,2},{7,3},{8,12},{9,13},{10,... | collective-permute-start | bytes 442376 | tf_op jit(solution)/shard_map/ppermute | solution.py:282
  42.8 2.9 %collective-permute-done.21 = bf16[2,2,48,384]{3,2,0,1:T(8,128)(2,1)S(1)} collective-permute-done((bf16[2,2,48,384]{3,2,0,1:T(8,128)(2,1)S(1)}, bf16[2,2,48,384]{3,2,0,1:T(8,128)(2,1)S(1)}, u32[]{:S(2)}, u32[]{:S(2)}) %collective-permute-start.21) | collective-permute-done | bytes 147488 | tf_op jit(solution)/shard_map/ppermute | solution.py:282
  45.6 1.2 collective-permute-start.3
  46.9 5.0 %collective-permute-start.4 = (bf16[2,2,48,384]{3,2,0,1:T(8,128)(2,1)S(1)}, bf16[2,2,48,384]{3,2,0,1:T(8,128)(2,1)S(1)}, u32[]{:S(2)}, u32[]{:S(2)}) collective-permute-start(bf16[2,2,48,384]{3,2,0,1:T(8,128)(2,1)S(1)} %pad_maximum_fusion.4), channel_id=1, source_target_pairs={{0,8},{1,9},{2,10},{3,11},{4,12},{5,13},{6,14},{7,15},{8,0},{9,1},... | collective-permute-start | bytes 442376 | tf_op jit(solution)/shard_map/ppermute | solution.py:282
  51.9 11.3 %collective-permute-start.5 = (bf16[2,2,48,384]{3,2,0,1:T(8,128)(2,1)S(1)}, bf16[2,2,48,384]{3,2,0,1:T(8,128)(2,1)S(1)}, u32[]{:S(2)}, u32[]{:S(2)}) collective-permute-start(bf16[2,2,48,384]{3,2,0,1:T(8,128)(2,1)S(1)} %pad_maximum_fusion.5), channel_id=1, source_target_pairs={{0,10},{1,11},{2,8},{3,9},{4,14},{5,15},{6,12},{7,13},{8,2},{9,3},... | collective-permute-start | bytes 442376 | tf_op jit(solution)/shard_map/ppermute | solution.py:282
  63.3 4.4 %collective-permute-start.7 = (bf16[2,2,48,384]{3,2,1,0:T(8,128)(2,1)S(1)}, bf16[2,2,48,384]{3,2,1,0:T(8,128)(2,1)S(1)}, u32[]{:S(2)}, u32[]{:S(2)}) collective-permute-start(bf16[2,2,48,384]{3,2,1,0:T(8,128)(2,1)S(1)} %pad_maximum_fusion.7), channel_id=1, source_target_pairs={{0,14},{1,15},{2,12},{3,13},{4,10},{5,11},{6,8},{7,9},{8,6},{9,7},... | collective-permute-start | bytes 442376 | tf_op jit(solution)/shard_map/ppermute | solution.py:282
  67.7 5.3 %mix_modes.3 = (bf16[8,2,48,384]{3,2,1,0:T(8,128)(2,1)S(1)}, bf16[8,2,48,384]{3,2,1,0:T(8,128)(2,1)S(1)}) custom-call(s32[1]{0:T(128)} %bitcast.place, bf16[2,2,48,384]{3,2,1,0:T(8,128)(2,1)S(1)} %copy.28.refs_0_, bf16[2,2,48,384]{3,2,1,0:T(8,128)(2,1)S(1)} %copy.29.refs_1_, bf16[2,2,48,384]{3,2,1,0:T(8,128)(2,1)S(1)} %copy.30.refs_2_, ...), custom_call_target="tpu_custom_call" | custom-call | flops 3623878656 | bytes 4718592 | tf_op jit(solution)/shard_map/mix_modes/pallas_call | solution.py:149
  73.3 5.5 %mix_modes.2 = (bf16[8,2,48,384]{3,2,1,0:T(8,128)(2,1)S(1)}, bf16[8,2,48,384]{3,2,1,0:T(8,128)(2,1)S(1)}) custom-call(s32[1]{0:T(128)} %bitcast.place, bf16[2,2,48,384]{3,2,1,0:T(8,128)(2,1)S(1)} %copy.20.refs_0_, bf16[2,2,48,384]{3,2,1,0:T(8,128)(2,1)S(1)} %copy.21.refs_1_, bf16[2,2,48,384]{3,2,1,0:T(8,128)(2,1)S(1)} %copy.22.refs_2_, ...), custom_call_target="tpu_custom_call" | custom-call | flops 3623878656 | bytes 4718592 | tf_op jit(solution)/shard_map/mix_modes/pallas_call | solution.py:149
  80.4 3.0 %collective-permute-start.26 = (bf16[2,2,48,384]{3,2,0,1:T(8,128)(2,1)S(1)}, bf16[2,2,48,384]{3,2,0,1:T(8,128)(2,1)S(1)}, u32[]{:S(2)}, u32[]{:S(2)}) collective-permute-start(bf16[2,2,48,384]{3,2,0,1:T(8,128)(2,1)S(1)} %pad_maximum_fusion.26), channel_id=1, source_target_pairs={{0,4},{1,5},{2,6},{3,7},{4,0},{5,1},{6,2},{7,3},{8,12},{9,13},{10,... | collective-permute-start | bytes 442376 | tf_op jit(solution)/shard_map/ppermute | solution.py:282
  84.4 4.0 %collective-permute-start.28 = (bf16[2,2,48,384]{3,2,0,1:T(8,128)(2,1)S(1)}, bf16[2,2,48,384]{3,2,0,1:T(8,128)(2,1)S(1)}, u32[]{:S(2)}, u32[]{:S(2)}) collective-permute-start(bf16[2,2,48,384]{3,2,0,1:T(8,128)(2,1)S(1)} %pad_maximum_fusion.28), channel_id=1, source_target_pairs={{0,8},{1,9},{2,10},{3,11},{4,12},{5,13},{6,14},{7,15},{8,0},{9,1},... | collective-permute-start | bytes 442376 | tf_op jit(solution)/shard_map/ppermute | solution.py:282
  88.9 2.4 %collective-permute-start.30 = (bf16[2,2,48,384]{3,2,0,1:T(8,128)(2,1)S(1)}, bf16[2,2,48,384]{3,2,0,1:T(8,128)(2,1)S(1)}, u32[]{:S(2)}, u32[]{:S(2)}) collective-permute-start(bf16[2,2,48,384]{3,2,0,1:T(8,128)(2,1)S(1)} %pad_maximum_fusion.30), channel_id=1, source_target_pairs={{0,12},{1,13},{2,14},{3,15},{4,8},{5,9},{6,10},{7,11},{8,4},{9,5},... | collective-permute-start | bytes 442376 | tf_op jit(solution)/shard_map/ppermute | solution.py:282
  91.3 4.9 %collective-permute-start.31 = (bf16[2,2,48,384]{3,2,1,0:T(8,128)(2,1)S(1)}, bf16[2,2,48,384]{3,2,1,0:T(8,128)(2,1)S(1)}, u32[]{:S(2)}, u32[]{:S(2)}) collective-permute-start(bf16[2,2,48,384]{3,2,1,0:T(8,128)(2,1)S(1)} %pad_maximum_fusion.31), channel_id=1, source_target_pairs={{0,14},{1,15},{2,12},{3,13},{4,10},{5,11},{6,8},{7,9},{8,6},{9,7},... | collective-permute-start | bytes 442376 | tf_op jit(solution)/shard_map/ppermute | solution.py:282
  97.2 8.0 %collective-permute-start.10 = (bf16[2,2,48,384]{3,2,0,1:T(8,128)(2,1)S(1)}, bf16[2,2,48,384]{3,2,0,1:T(8,128)(2,1)S(1)}, u32[]{:S(2)}, u32[]{:S(2)}) collective-permute-start(bf16[2,2,48,384]{3,2,0,1:T(8,128)(2,1)S(1)} %pad_maximum_fusion.10), channel_id=1, source_target_pairs={{0,4},{1,5},{2,6},{3,7},{4,0},{5,1},{6,2},{7,3},{8,12},{9,13},{10,... | collective-permute-start | bytes 442376 | tf_op jit(solution)/shard_map/ppermute | solution.py:282
  105.4 4.5 %collective-permute-done.29 = bf16[2,2,48,384]{3,2,0,1:T(8,128)(2,1)S(1)} collective-permute-done((bf16[2,2,48,384]{3,2,0,1:T(8,128)(2,1)S(1)}, bf16[2,2,48,384]{3,2,0,1:T(8,128)(2,1)S(1)}, u32[]{:S(2)}, u32[]{:S(2)}) %collective-permute-start.29) | collective-permute-done | bytes 147488 | tf_op jit(solution)/shard_map/ppermute | solution.py:282
  109.9 3.7 %collective-permute-start.12 = (bf16[2,2,48,384]{3,2,0,1:T(8,128)(2,1)S(1)}, bf16[2,2,48,384]{3,2,0,1:T(8,128)(2,1)S(1)}, u32[]{:S(2)}, u32[]{:S(2)}) collective-permute-start(bf16[2,2,48,384]{3,2,0,1:T(8,128)(2,1)S(1)} %pad_maximum_fusion.12), channel_id=1, source_target_pairs={{0,8},{1,9},{2,10},{3,11},{4,12},{5,13},{6,14},{7,15},{8,0},{9,1},... | collective-permute-start | bytes 442376 | tf_op jit(solution)/shard_map/ppermute | solution.py:282
  113.6 7.6 %collective-permute-start.13 = (bf16[2,2,48,384]{3,2,0,1:T(8,128)(2,1)S(1)}, bf16[2,2,48,384]{3,2,0,1:T(8,128)(2,1)S(1)}, u32[]{:S(2)}, u32[]{:S(2)}) collective-permute-start(bf16[2,2,48,384]{3,2,0,1:T(8,128)(2,1)S(1)} %pad_maximum_fusion.13), channel_id=1, source_target_pairs={{0,10},{1,11},{2,8},{3,9},{4,14},{5,15},{6,12},{7,13},{8,2},{9,3},... | collective-permute-start | bytes 442376 | tf_op jit(solution)/shard_map/ppermute | solution.py:282
  121.3 2.7 %collective-permute-start.14 = (bf16[2,2,48,384]{3,2,0,1:T(8,128)(2,1)S(1)}, bf16[2,2,48,384]{3,2,0,1:T(8,128)(2,1)S(1)}, u32[]{:S(2)}, u32[]{:S(2)}) collective-permute-start(bf16[2,2,48,384]{3,2,0,1:T(8,128)(2,1)S(1)} %pad_maximum_fusion.14), channel_id=1, source_target_pairs={{0,12},{1,13},{2,14},{3,15},{4,8},{5,9},{6,10},{7,11},{8,4},{9,5},... | collective-permute-start | bytes 442376 | tf_op jit(solution)/shard_map/ppermute | solution.py:282
  124.0 4.4 %collective-permute-start.15 = (bf16[2,2,48,384]{3,2,1,0:T(8,128)(2,1)S(1)}, bf16[2,2,48,384]{3,2,1,0:T(8,128)(2,1)S(1)}, u32[]{:S(2)}, u32[]{:S(2)}) collective-permute-start(bf16[2,2,48,384]{3,2,1,0:T(8,128)(2,1)S(1)} %pad_maximum_fusion.15), channel_id=1, source_target_pairs={{0,14},{1,15},{2,12},{3,13},{4,10},{5,11},{6,8},{7,9},{8,6},{9,7},... | collective-permute-start | bytes 442376 | tf_op jit(solution)/shard_map/ppermute | solution.py:282
  128.4 18.6 %channel_mlp.2.refs_18_ = bf16[4,3,180,768]{3,2,1,0:T(8,128)(2,1)S(1)} custom-call(s32[1]{0:T(128)} %bitcast.place, bf16[2,2,48,384]{3,2,1,0:T(8,128)(2,1)S(1)} %copy.35.refs_0_, bf16[2,2,48,384]{3,2,1,0:T(8,128)(2,1)S(1)} %copy.36.refs_1_, bf16[2,2,48,384]{3,2,1,0:T(8,128)(2,1)S(1)} %copy.37.refs_2_, bf16[2,2,48,384]{3,2,1,0:T(8,128)(2,1)S(1)} %copy.38.refs_3_, ...), custom_call_target="tpu_custom_call" | custom-call | flops 10192158720 | bytes 12754944 | tf_op jit(solution)/shard_map/channel_mlp/pallas_call | solution.py:230
  147.2 18.8 %channel_mlp.3 = bf16[4,3,180,768]{3,2,1,0:T(8,128)(2,1)S(1)} custom-call(s32[1]{0:T(128)} %bitcast.place, bf16[2,2,48,384]{3,2,1,0:T(8,128)(2,1)S(1)} %copy.43.refs_0_, bf16[2,2,48,384]{3,2,1,0:T(8,128)(2,1)S(1)} %copy.44.refs_1_, bf16[2,2,48,384]{3,2,1,0:T(8,128)(2,1)S(1)} %copy.45.refs_2_, ...), custom_call_target="tpu_custom_call", output_to_operand_aliasing={{}: (19, {})} | custom-call | flops 10192158720 | bytes 12754944 | tf_op jit(solution)/shard_map/channel_mlp/pallas_call | solution.py:230
  166.0 3.0 %copy.51 = bf16[4,3,180,768]{3,0,2,1:T(4,128)(2,1)} copy(bf16[4,3,180,768]{3,2,1,0:T(8,128)(2,1)S(1)} %channel_mlp.3) | data formatting | bytes 6635520 | tf_op jit(solution)/shard_map/channel_mlp/pallas_call | solution.py:230
  (163 shorter events, 14.5 us)
Async XLA Ops:
  7.3 8.0 %collective-permute-start.16 = (bf16[8,2,48,384]{3,2,1,0:T(8,128)(2,1)}, bf16[8,2,48,384]{3,2,1,0:T(8,128)(2,1)}, u32[]{:S(2)}, u32[]{:S(2)}) collective-permute-start(bf16[8,2,48,384]{3,2,1,0:T(8,128)(2,1)} %get-tuple-element.18), channel_id=1, source_target_pairs={{0,1},{1,0},{2,3},{3,2},{4,5},{5,4},{6,7},{7,6},{8,9},{9,8},{10,11... | collective-permute-start | bytes 1769480 | tf_op jit(solution)/shard_map/ppermute | solution.py:274
  11.3 13.3 %collective-permute-start = (bf16[8,2,48,384]{3,2,1,0:T(8,128)(2,1)}, bf16[8,2,48,384]{3,2,1,0:T(8,128)(2,1)}, u32[]{:S(2)}, u32[]{:S(2)}) collective-permute-start(bf16[8,2,48,384]{3,2,1,0:T(8,128)(2,1)} %get-tuple-element.14), channel_id=1, source_target_pairs={{0,1},{1,0},{2,3},{3,2},{4,5},{5,4},{6,7},{7,6},{8,9},{9,8},{10,11... | collective-permute-start | bytes 1769480 | tf_op jit(solution)/shard_map/ppermute | solution.py:274
  16.6 10.7 %collective-permute-start.17 = (bf16[2,2,48,384]{3,2,0,1:T(8,128)(2,1)S(1)}, bf16[2,2,48,384]{3,2,0,1:T(8,128)(2,1)S(1)}, u32[]{:S(2)}, u32[]{:S(2)}) collective-permute-start(bf16[2,2,48,384]{3,2,0,1:T(8,128)(2,1)S(1)} %pad_maximum_fusion.17), channel_id=1, source_target_pairs={{0,2},{1,3},{2,0},{3,1},{4,6},{5,7},{6,4},{7,5},{8,10},{9,11},{10,... | collective-permute-start | bytes 442376 | tf_op jit(solution)/shard_map/ppermute | solution.py:282
  19.6 11.9 %collective-permute-start.18 = (bf16[2,2,48,384]{3,2,0,1:T(8,128)(2,1)S(1)}, bf16[2,2,48,384]{3,2,0,1:T(8,128)(2,1)S(1)}, u32[]{:S(2)}, u32[]{:S(2)}) collective-permute-start(bf16[2,2,48,384]{3,2,0,1:T(8,128)(2,1)S(1)} %pad_maximum_fusion.18), channel_id=1, source_target_pairs={{0,4},{1,5},{2,6},{3,7},{4,0},{5,1},{6,2},{7,3},{8,12},{9,13},{10,... | collective-permute-start | bytes 442376 | tf_op jit(solution)/shard_map/ppermute | solution.py:282
  21.3 11.6 %collective-permute-start.19 = (bf16[2,2,48,384]{3,2,0,1:T(8,128)(2,1)S(1)}, bf16[2,2,48,384]{3,2,0,1:T(8,128)(2,1)S(1)}, u32[]{:S(2)}, u32[]{:S(2)}) collective-permute-start(bf16[2,2,48,384]{3,2,0,1:T(8,128)(2,1)S(1)} %pad_maximum_fusion.19), channel_id=1, source_target_pairs={{0,6},{1,7},{2,4},{3,5},{4,2},{5,3},{6,0},{7,1},{8,14},{9,15},{10,... | collective-permute-start | bytes 442376 | tf_op jit(solution)/shard_map/ppermute | solution.py:282
  21.4 13.8 %collective-permute-start.20 = (bf16[2,2,48,384]{3,2,0,1:T(8,128)(2,1)S(1)}, bf16[2,2,48,384]{3,2,0,1:T(8,128)(2,1)S(1)}, u32[]{:S(2)}, u32[]{:S(2)}) collective-permute-start(bf16[2,2,48,384]{3,2,0,1:T(8,128)(2,1)S(1)} %pad_maximum_fusion.20), channel_id=1, source_target_pairs={{0,8},{1,9},{2,10},{3,11},{4,12},{5,13},{6,14},{7,15},{8,0},{9,1},... | collective-permute-start | bytes 442376 | tf_op jit(solution)/shard_map/ppermute | solution.py:282
  24.5 21.1 %collective-permute-start.21 = (bf16[2,2,48,384]{3,2,0,1:T(8,128)(2,1)S(1)}, bf16[2,2,48,384]{3,2,0,1:T(8,128)(2,1)S(1)}, u32[]{:S(2)}, u32[]{:S(2)}) collective-permute-start(bf16[2,2,48,384]{3,2,0,1:T(8,128)(2,1)S(1)} %pad_maximum_fusion.21), channel_id=1, source_target_pairs={{0,10},{1,11},{2,8},{3,9},{4,14},{5,15},{6,12},{7,13},{8,2},{9,3},... | collective-permute-start | bytes 442376 | tf_op jit(solution)/shard_map/ppermute | solution.py:282
  27.3 19.6 %collective-permute-start.22 = (bf16[2,2,48,384]{3,2,0,1:T(8,128)(2,1)S(1)}, bf16[2,2,48,384]{3,2,0,1:T(8,128)(2,1)S(1)}, u32[]{:S(2)}, u32[]{:S(2)}) collective-permute-start(bf16[2,2,48,384]{3,2,0,1:T(8,128)(2,1)S(1)} %pad_maximum_fusion.22), channel_id=1, source_target_pairs={{0,12},{1,13},{2,14},{3,15},{4,8},{5,9},{6,10},{7,11},{8,4},{9,5},... | collective-permute-start | bytes 442376 | tf_op jit(solution)/shard_map/ppermute | solution.py:282
  31.5 20.4 %collective-permute-start.23 = (bf16[2,2,48,384]{3,2,1,0:T(8,128)(2,1)S(1)}, bf16[2,2,48,384]{3,2,1,0:T(8,128)(2,1)S(1)}, u32[]{:S(2)}, u32[]{:S(2)}) collective-permute-start(bf16[2,2,48,384]{3,2,1,0:T(8,128)(2,1)S(1)} %pad_maximum_fusion.23), channel_id=1, source_target_pairs={{0,14},{1,15},{2,12},{3,13},{4,10},{5,11},{6,8},{7,9},{8,6},{9,7},... | collective-permute-start | bytes 442376 | tf_op jit(solution)/shard_map/ppermute | solution.py:282
  32.8 30.3 %collective-permute-start.1 = (bf16[2,2,48,384]{3,2,0,1:T(8,128)(2,1)S(1)}, bf16[2,2,48,384]{3,2,0,1:T(8,128)(2,1)S(1)}, u32[]{:S(2)}, u32[]{:S(2)}) collective-permute-start(bf16[2,2,48,384]{3,2,0,1:T(8,128)(2,1)S(1)} %pad_maximum_fusion.1), channel_id=1, source_target_pairs={{0,2},{1,3},{2,0},{3,1},{4,6},{5,7},{6,4},{7,5},{8,10},{9,11},{10,... | collective-permute-start | bytes 442376 | tf_op jit(solution)/shard_map/ppermute | solution.py:282
  35.2 28.1 %collective-permute-start.2 = (bf16[2,2,48,384]{3,2,0,1:T(8,128)(2,1)S(1)}, bf16[2,2,48,384]{3,2,0,1:T(8,128)(2,1)S(1)}, u32[]{:S(2)}, u32[]{:S(2)}) collective-permute-start(bf16[2,2,48,384]{3,2,0,1:T(8,128)(2,1)S(1)} %pad_maximum_fusion.2), channel_id=1, source_target_pairs={{0,4},{1,5},{2,6},{3,7},{4,0},{5,1},{6,2},{7,3},{8,12},{9,13},{10,... | collective-permute-start | bytes 442376 | tf_op jit(solution)/shard_map/ppermute | solution.py:282
  45.6 27.4 %collective-permute-start.3 = (bf16[2,2,48,384]{3,2,0,1:T(8,128)(2,1)S(1)}, bf16[2,2,48,384]{3,2,0,1:T(8,128)(2,1)S(1)}, u32[]{:S(2)}, u32[]{:S(2)}) collective-permute-start(bf16[2,2,48,384]{3,2,0,1:T(8,128)(2,1)S(1)} %pad_maximum_fusion.3), channel_id=1, source_target_pairs={{0,6},{1,7},{2,4},{3,5},{4,2},{5,3},{6,0},{7,1},{8,14},{9,15},{10,... | collective-permute-start | bytes 442376 | tf_op jit(solution)/shard_map/ppermute | solution.py:282
  46.9 26.3 %collective-permute-start.4 = (bf16[2,2,48,384]{3,2,0,1:T(8,128)(2,1)S(1)}, bf16[2,2,48,384]{3,2,0,1:T(8,128)(2,1)S(1)}, u32[]{:S(2)}, u32[]{:S(2)}) collective-permute-start(bf16[2,2,48,384]{3,2,0,1:T(8,128)(2,1)S(1)} %pad_maximum_fusion.4), channel_id=1, source_target_pairs={{0,8},{1,9},{2,10},{3,11},{4,12},{5,13},{6,14},{7,15},{8,0},{9,1},... | collective-permute-start | bytes 442376 | tf_op jit(solution)/shard_map/ppermute | solution.py:282
  51.9 21.3 %collective-permute-start.5 = (bf16[2,2,48,384]{3,2,0,1:T(8,128)(2,1)S(1)}, bf16[2,2,48,384]{3,2,0,1:T(8,128)(2,1)S(1)}, u32[]{:S(2)}, u32[]{:S(2)}) collective-permute-start(bf16[2,2,48,384]{3,2,0,1:T(8,128)(2,1)S(1)} %pad_maximum_fusion.5), channel_id=1, source_target_pairs={{0,10},{1,11},{2,8},{3,9},{4,14},{5,15},{6,12},{7,13},{8,2},{9,3},... | collective-permute-start | bytes 442376 | tf_op jit(solution)/shard_map/ppermute | solution.py:282
  63.2 10.1 %collective-permute-start.6 = (bf16[2,2,48,384]{3,2,0,1:T(8,128)(2,1)S(1)}, bf16[2,2,48,384]{3,2,0,1:T(8,128)(2,1)S(1)}, u32[]{:S(2)}, u32[]{:S(2)}) collective-permute-start(bf16[2,2,48,384]{3,2,0,1:T(8,128)(2,1)S(1)} %pad_maximum_fusion.6), channel_id=1, source_target_pairs={{0,12},{1,13},{2,14},{3,15},{4,8},{5,9},{6,10},{7,11},{8,4},{9,5},... | collective-permute-start | bytes 442376 | tf_op jit(solution)/shard_map/ppermute | solution.py:282
  63.3 10.0 %collective-permute-start.7 = (bf16[2,2,48,384]{3,2,1,0:T(8,128)(2,1)S(1)}, bf16[2,2,48,384]{3,2,1,0:T(8,128)(2,1)S(1)}, u32[]{:S(2)}, u32[]{:S(2)}) collective-permute-start(bf16[2,2,48,384]{3,2,1,0:T(8,128)(2,1)S(1)} %pad_maximum_fusion.7), channel_id=1, source_target_pairs={{0,14},{1,15},{2,12},{3,13},{4,10},{5,11},{6,8},{7,9},{8,6},{9,7},... | collective-permute-start | bytes 442376 | tf_op jit(solution)/shard_map/ppermute | solution.py:282
  73.1 6.4 %collective-permute-start.24 = (bf16[8,2,48,384]{3,2,1,0:T(8,128)(2,1)S(1)}, bf16[8,2,48,384]{3,2,1,0:T(8,128)(2,1)S(1)}, u32[]{:S(2)}, u32[]{:S(2)}) collective-permute-start(bf16[8,2,48,384]{3,2,1,0:T(8,128)(2,1)S(1)} %get-tuple-element.20), channel_id=1, source_target_pairs={{0,1},{1,0},{2,3},{3,2},{4,5},{5,4},{6,7},{7,6},{8,9},{9,8},{10,11... | collective-permute-start | bytes 1769480 | tf_op jit(solution)/shard_map/ppermute | solution.py:274
  78.8 9.7 %collective-permute-start.8 = (bf16[8,2,48,384]{3,2,1,0:T(8,128)(2,1)S(1)}, bf16[8,2,48,384]{3,2,1,0:T(8,128)(2,1)S(1)}, u32[]{:S(2)}, u32[]{:S(2)}) collective-permute-start(bf16[8,2,48,384]{3,2,1,0:T(8,128)(2,1)S(1)} %get-tuple-element.16), channel_id=1, source_target_pairs={{0,1},{1,0},{2,3},{3,2},{4,5},{5,4},{6,7},{7,6},{8,9},{9,8},{10,11... | collective-permute-start | bytes 1769480 | tf_op jit(solution)/shard_map/ppermute | solution.py:274
  79.6 9.3 %collective-permute-start.25 = (bf16[2,2,48,384]{3,2,0,1:T(8,128)(2,1)S(1)}, bf16[2,2,48,384]{3,2,0,1:T(8,128)(2,1)S(1)}, u32[]{:S(2)}, u32[]{:S(2)}) collective-permute-start(bf16[2,2,48,384]{3,2,0,1:T(8,128)(2,1)S(1)} %pad_maximum_fusion.25), channel_id=1, source_target_pairs={{0,2},{1,3},{2,0},{3,1},{4,6},{5,7},{6,4},{7,5},{8,10},{9,11},{10,... | collective-permute-start | bytes 442376 | tf_op jit(solution)/shard_map/ppermute | solution.py:282
  80.4 10.9 %collective-permute-start.26 = (bf16[2,2,48,384]{3,2,0,1:T(8,128)(2,1)S(1)}, bf16[2,2,48,384]{3,2,0,1:T(8,128)(2,1)S(1)}, u32[]{:S(2)}, u32[]{:S(2)}) collective-permute-start(bf16[2,2,48,384]{3,2,0,1:T(8,128)(2,1)S(1)} %pad_maximum_fusion.26), channel_id=1, source_target_pairs={{0,4},{1,5},{2,6},{3,7},{4,0},{5,1},{6,2},{7,3},{8,12},{9,13},{10,... | collective-permute-start | bytes 442376 | tf_op jit(solution)/shard_map/ppermute | solution.py:282
  83.4 13.4 %collective-permute-start.27 = (bf16[2,2,48,384]{3,2,0,1:T(8,128)(2,1)S(1)}, bf16[2,2,48,384]{3,2,0,1:T(8,128)(2,1)S(1)}, u32[]{:S(2)}, u32[]{:S(2)}) collective-permute-start(bf16[2,2,48,384]{3,2,0,1:T(8,128)(2,1)S(1)} %pad_maximum_fusion.27), channel_id=1, source_target_pairs={{0,6},{1,7},{2,4},{3,5},{4,2},{5,3},{6,0},{7,1},{8,14},{9,15},{10,... | collective-permute-start | bytes 442376 | tf_op jit(solution)/shard_map/ppermute | solution.py:282
  84.4 12.8 %collective-permute-start.28 = (bf16[2,2,48,384]{3,2,0,1:T(8,128)(2,1)S(1)}, bf16[2,2,48,384]{3,2,0,1:T(8,128)(2,1)S(1)}, u32[]{:S(2)}, u32[]{:S(2)}) collective-permute-start(bf16[2,2,48,384]{3,2,0,1:T(8,128)(2,1)S(1)} %pad_maximum_fusion.28), channel_id=1, source_target_pairs={{0,8},{1,9},{2,10},{3,11},{4,12},{5,13},{6,14},{7,15},{8,0},{9,1},... | collective-permute-start | bytes 442376 | tf_op jit(solution)/shard_map/ppermute | solution.py:282
  88.5 21.3 %collective-permute-start.29 = (bf16[2,2,48,384]{3,2,0,1:T(8,128)(2,1)S(1)}, bf16[2,2,48,384]{3,2,0,1:T(8,128)(2,1)S(1)}, u32[]{:S(2)}, u32[]{:S(2)}) collective-permute-start(bf16[2,2,48,384]{3,2,0,1:T(8,128)(2,1)S(1)} %pad_maximum_fusion.29), channel_id=1, source_target_pairs={{0,10},{1,11},{2,8},{3,9},{4,14},{5,15},{6,12},{7,13},{8,2},{9,3},... | collective-permute-start | bytes 442376 | tf_op jit(solution)/shard_map/ppermute | solution.py:282
  88.9 21.0 %collective-permute-start.30 = (bf16[2,2,48,384]{3,2,0,1:T(8,128)(2,1)S(1)}, bf16[2,2,48,384]{3,2,0,1:T(8,128)(2,1)S(1)}, u32[]{:S(2)}, u32[]{:S(2)}) collective-permute-start(bf16[2,2,48,384]{3,2,0,1:T(8,128)(2,1)S(1)} %pad_maximum_fusion.30), channel_id=1, source_target_pairs={{0,12},{1,13},{2,14},{3,15},{4,8},{5,9},{6,10},{7,11},{8,4},{9,5},... | collective-permute-start | bytes 442376 | tf_op jit(solution)/shard_map/ppermute | solution.py:282
  91.3 22.3 %collective-permute-start.31 = (bf16[2,2,48,384]{3,2,1,0:T(8,128)(2,1)S(1)}, bf16[2,2,48,384]{3,2,1,0:T(8,128)(2,1)S(1)}, u32[]{:S(2)}, u32[]{:S(2)}) collective-permute-start(bf16[2,2,48,384]{3,2,1,0:T(8,128)(2,1)S(1)} %pad_maximum_fusion.31), channel_id=1, source_target_pairs={{0,14},{1,15},{2,12},{3,13},{4,10},{5,11},{6,8},{7,9},{8,6},{9,7},... | collective-permute-start | bytes 442376 | tf_op jit(solution)/shard_map/ppermute | solution.py:282
  96.8 24.5 %collective-permute-start.9 = (bf16[2,2,48,384]{3,2,0,1:T(8,128)(2,1)S(1)}, bf16[2,2,48,384]{3,2,0,1:T(8,128)(2,1)S(1)}, u32[]{:S(2)}, u32[]{:S(2)}) collective-permute-start(bf16[2,2,48,384]{3,2,0,1:T(8,128)(2,1)S(1)} %pad_maximum_fusion.9), channel_id=1, source_target_pairs={{0,2},{1,3},{2,0},{3,1},{4,6},{5,7},{6,4},{7,5},{8,10},{9,11},{10,... | collective-permute-start | bytes 442376 | tf_op jit(solution)/shard_map/ppermute | solution.py:282
  97.2 26.8 %collective-permute-start.10 = (bf16[2,2,48,384]{3,2,0,1:T(8,128)(2,1)S(1)}, bf16[2,2,48,384]{3,2,0,1:T(8,128)(2,1)S(1)}, u32[]{:S(2)}, u32[]{:S(2)}) collective-permute-start(bf16[2,2,48,384]{3,2,0,1:T(8,128)(2,1)S(1)} %pad_maximum_fusion.10), channel_id=1, source_target_pairs={{0,4},{1,5},{2,6},{3,7},{4,0},{5,1},{6,2},{7,3},{8,12},{9,13},{10,... | collective-permute-start | bytes 442376 | tf_op jit(solution)/shard_map/ppermute | solution.py:282
  109.9 37.2 %collective-permute-start.11 = (bf16[2,2,48,384]{3,2,0,1:T(8,128)(2,1)S(1)}, bf16[2,2,48,384]{3,2,0,1:T(8,128)(2,1)S(1)}, u32[]{:S(2)}, u32[]{:S(2)}) collective-permute-start(bf16[2,2,48,384]{3,2,0,1:T(8,128)(2,1)S(1)} %pad_maximum_fusion.11), channel_id=1, source_target_pairs={{0,6},{1,7},{2,4},{3,5},{4,2},{5,3},{6,0},{7,1},{8,14},{9,15},{10,... | collective-permute-start | bytes 442376 | tf_op jit(solution)/shard_map/ppermute | solution.py:282
  109.9 37.2 %collective-permute-start.12 = (bf16[2,2,48,384]{3,2,0,1:T(8,128)(2,1)S(1)}, bf16[2,2,48,384]{3,2,0,1:T(8,128)(2,1)S(1)}, u32[]{:S(2)}, u32[]{:S(2)}) collective-permute-start(bf16[2,2,48,384]{3,2,0,1:T(8,128)(2,1)S(1)} %pad_maximum_fusion.12), channel_id=1, source_target_pairs={{0,8},{1,9},{2,10},{3,11},{4,12},{5,13},{6,14},{7,15},{8,0},{9,1},... | collective-permute-start | bytes 442376 | tf_op jit(solution)/shard_map/ppermute | solution.py:282
  113.6 33.5 %collective-permute-start.13 = (bf16[2,2,48,384]{3,2,0,1:T(8,128)(2,1)S(1)}, bf16[2,2,48,384]{3,2,0,1:T(8,128)(2,1)S(1)}, u32[]{:S(2)}, u32[]{:S(2)}) collective-permute-start(bf16[2,2,48,384]{3,2,0,1:T(8,128)(2,1)S(1)} %pad_maximum_fusion.13), channel_id=1, source_target_pairs={{0,10},{1,11},{2,8},{3,9},{4,14},{5,15},{6,12},{7,13},{8,2},{9,3},... | collective-permute-start | bytes 442376 | tf_op jit(solution)/shard_map/ppermute | solution.py:282
  121.3 25.9 %collective-permute-start.14 = (bf16[2,2,48,384]{3,2,0,1:T(8,128)(2,1)S(1)}, bf16[2,2,48,384]{3,2,0,1:T(8,128)(2,1)S(1)}, u32[]{:S(2)}, u32[]{:S(2)}) collective-permute-start(bf16[2,2,48,384]{3,2,0,1:T(8,128)(2,1)S(1)} %pad_maximum_fusion.14), channel_id=1, source_target_pairs={{0,12},{1,13},{2,14},{3,15},{4,8},{5,9},{6,10},{7,11},{8,4},{9,5},... | collective-permute-start | bytes 442376 | tf_op jit(solution)/shard_map/ppermute | solution.py:282
  124.0 23.2 %collective-permute-start.15 = (bf16[2,2,48,384]{3,2,1,0:T(8,128)(2,1)S(1)}, bf16[2,2,48,384]{3,2,1,0:T(8,128)(2,1)S(1)}, u32[]{:S(2)}, u32[]{:S(2)}) collective-permute-start(bf16[2,2,48,384]{3,2,1,0:T(8,128)(2,1)S(1)} %pad_maximum_fusion.15), channel_id=1, source_target_pairs={{0,14},{1,15},{2,12},{3,13},{4,10},{5,11},{6,8},{7,9},{8,6},{9,7},... | collective-permute-start | bytes 442376 | tf_op jit(solution)/shard_map/ppermute | solution.py:282
  (17 other events, 202.6 us)
